TPU v7x, 512 devices: a whole 4x8x8 slice. The times are simulated.
512 devices in a mesh: pw: 128 (over x, z_lo, y), band: 4 (over z_hi, core).
Axes of the slice: x: 4, y: 8, z: 8 (z_hi: 2, z_lo: 4; z = z_hi * 4 + z_lo), core: 2. Of those that a mesh axis runs over, the one named last changes fastest.
Arguments:
- orbitals: bfloat16 [163840, 512], P('pw', 'band'), may hold values from -0.296875 to 0.296875
- exchange_vectors: bfloat16 [163840, 2048], P('pw', 'band'), may hold values from -0.296875 to 0.296875
- cotangent: bfloat16 [163840, 512], P('pw', 'band'), may hold values from -0.1875 to 0.1875
Outputs:
- orbital_grad: bfloat16 [163840, 512], P('pw', 'band')
- vector_grad: bfloat16 [163840, 2048], P('pw', 'band')
All inputs are finite; a program needn't handle non-finite values.
Results may differ from a plain program's by a relative error of at most 0.013.
Values may be sent and summed in bfloat16 or wider, within the bound.
A program may use at most 64 MiB of HBM per device.

v0:
```python
import jax
import jax.numpy as jnp
from jax import lax
from jax.sharding import PartitionSpec as P


def contract_rows(left, right):
    return lax.dot_general(
        left, right, (((0,), (0,)), ((), ())), preferred_element_type=jnp.float32
    )


def contract_cols(left, right):
    return lax.dot_general(
        left, right, (((1,), (1,)), ((), ())), preferred_element_type=jnp.float32
    )


def body(orbitals, exchange_vectors, cotangent):
    panel_orbitals, panel_cotangent = (
        lax.all_gather(orbitals, "band", axis=1, tiled=True),
        lax.all_gather(cotangent, "band", axis=1, tiled=True),
    )
    panel_width = panel_orbitals.shape[1]
    partial_terms = jnp.concatenate(
        [
            contract_rows(exchange_vectors, panel_orbitals),
            contract_rows(exchange_vectors, panel_cotangent),
        ],
        axis=1,
    )
    summed = lax.psum(partial_terms, "pw").astype(jnp.bfloat16)
    projections = summed[:, :panel_width]
    cotangent_proj = summed[:, panel_width:]
    vector_grad = (
        contract_cols(panel_cotangent, projections) + contract_cols(panel_orbitals, cotangent_proj)
    ).astype(jnp.bfloat16)
    local_terms = jnp.dot(exchange_vectors, cotangent_proj, preferred_element_type=jnp.float32)
    orbital_grad = lax.psum_scatter(
        local_terms.astype(jnp.bfloat16), "band", scatter_dimension=1, tiled=True
    )
    return (orbital_grad, vector_grad)


def solution(mesh):
    placed = (P("pw", "band"), P("pw", "band"), P("pw", "band"))
    return jax.shard_map(
        body,
        mesh=mesh,
        in_specs=placed,
        out_specs=(P("pw", "band"), P("pw", "band")),
        check_vma=False,
    )
```

profile of v0, /device:TPU:1, one launch (start us, length us, event | category | flops | bytes accessed | tf_op | source)
XLA Modules:
  0.0 890.4 jit_solution(14413472509010651206)
XLA Ops:
  7.2 0.0 copy-start
  7.2 0.0 all-gather.5.cloned.1.call-start
  7.2 0.7 all-gather.5.cloned.1.call-update
  7.9 0.0 all-gather.3.cloned.1.call-start
  8.0 0.7 all-gather.3.cloned.1.call-update
  8.7 0.0 reduce-scatter.2.cloned.1.call-start
  8.7 45.2 %all-gather.5.cloned.1.call-done = bf16[1280,512]{1,0:T(8,128)(2,1)} async-done(((bf16[1280,128]{1,0:T(8,128)(2,1)}), bf16[1280,512]{1,0:T(8,128)(2,1)}) %all-gather.5.cloned.1.call-update) | async-done | bytes 1310736 | tf_op jit(solution)/shard_map/all_gather | solution.py:22
  53.9 0.0 copy-done
  53.9 3.2 fusion.8
  57.1 33.0 %all-gather.3.cloned.1.call-done = bf16[1280,512]{1,0:T(8,128)(2,1)} async-done(((bf16[1280,128]{1,0:T(8,128)(2,1)}), bf16[1280,512]{1,0:T(8,128)(2,1)}) %all-gather.3.cloned.1.call-update) | async-done | bytes 1310736 | tf_op jit(solution)/shard_map/all_gather | solution.py:21
  90.1 2.3 fusion.7
  92.4 0.0 copy-done.4
  92.4 0.2 pad_maximum_fusion
  92.6 633.4 %all-reduce.1 = bf16[512,1024]{0,1:T(8,128)(2,1)} all-reduce(f32[512,1024]{0,1:T(8,128)S(1)} %pad_maximum_fusion), channel_id=1, replica_groups=mesh['pw'=128,'band'=4] {'pw'}, use_global_device_ids=true, to_apply=%region_0.0 | all-reduce | flops 524288 | bytes 3145728 | tf_op jit(solution)/shard_map/psum | solution.py:32
  726.0 3.0 fusion.1
  729.0 0.0 reduce-scatter.2.cloned.1.call-update
  729.0 1.2 copy-done.1
  730.2 2.4 fusion.3
  732.6 0.0 copy-done.2
  732.6 0.0 copy-done.3
  732.6 0.9 fusion.2
  733.5 1.5 copy.6
  735.0 147.0 %reduce-scatter.2.cloned.1.call-done = bf16[1280,128]{0,1:T(8,128)(2,1)} async-done(((bf16[1280,512]{0,1:T(8,128)(2,1)}), bf16[1280,128]{0,1:T(8,128)(2,1)}) %reduce-scatter.2.cloned.1.call-update) | async-done | bytes 327696 | tf_op jit(solution)/shard_map/reduce_scatter | solution.py:39
  882.0 1.9 copy.5
  (4 shorter events, 0.0 us)
Async XLA Ops:
  7.2 46.8 %copy-start = (bf16[1280,512]{1,0:T(8,128)(2,1)S(1)}, bf16[1280,512]{1,0:T(8,128)(2,1)}, u32[]{:S(2)}) copy-start(bf16[1280,512]{1,0:T(8,128)(2,1)} %param.4) | copy-start | bytes 3932164
  7.2 46.7 %all-gather.5.cloned.1.call-start = ((), (), s32[]{:S(2)}) async-start(), calls=%async_computation.2 | async-start | bytes 1638400 | tf_op jit(solution)/shard_map/all_gather | solution.py:22
  7.9 82.2 %all-gather.3.cloned.1.call-start = ((), (), s32[]{:S(2)}) async-start(), calls=%async_computation.1 | async-start | bytes 1638400 | tf_op jit(solution)/shard_map/all_gather | solution.py:21
  8.7 873.3 %reduce-scatter.2.cloned.1.call-start = ((), (), s32[]{:S(2)}) async-start(), calls=%async_computation.3 | async-start | bytes 1638400 | tf_op jit(solution)/shard_map/reduce_scatter | solution.py:39
  90.1 2.3 copy-start.4
  729.0 1.2 copy-start.1
  730.2 2.4 copy-start.2
  730.2 2.4 copy-start.3
Sparse Core Ops, SparseCore 0:
  10.1 43.7 all-gather.4
  56.0 34.0 all-gather.2
  729.2 152.7 reduce-scatter.1
where the time goes:
time: 891 us; the launch traced here: 890 us
  blocking collectives  633 us (71%)
  waiting for transfers between devices  227 us (25%)
  between operations  13.8 us (2%)
  matrix products  11.7 us (1%)
    psum x1, blocking collectives, body(): summed = lax.psum(partial_terms, 'pw').astype(jnp.bfloat16)  633 us
    reduce_scatter x1, waiting for transfers between devices, body(): lax.psum_scatter(local_terms.astype(jnp.bfloat16), 'band', scatter_dimens...  147 us
    all_gather x1, waiting for transfers between devices, body(): lax.all_gather(cotangent, 'band', axis=1, tiled=True)  45.2 us
    all_gather x1, waiting for transfers between devices, body(): lax.all_gather(orbitals, 'band', axis=1, tiled=True)  33 us
  transfers between devices with their start and end apart: 3, of which 3 were waited for; matrix products, arithmetic and copies ran while one was open for 1% of the time, Pallas kernels for 0%

commit v1 on v0

v1 whole, which is shorter than its diff:
```python
import jax
import jax.numpy as jnp
from jax import lax
from jax.experimental import pallas as pl
from jax.experimental.pallas import tpu as pltpu
from jax.sharding import PartitionSpec as P

MESH = pl.DeviceIdType.MESH
BF, F32 = jnp.bfloat16, jnp.float32
NX, NY, NZ = 4, 8, 4
ROWS, HALF, NXI_DEV, LANES = 1280, 640, 512, 128
DMA = pltpu.SemaphoreType.DMA
CHUNKS = {"e": 512, "c0": 128, "c1": 128, "p0": 128, "p1": 128}
AR_BUFFERS = ("part", "rx", "sx", "ry", "sy", "rz", "full")
N_STAGES = 5


def dot_nn(left, right):
    return lax.dot_general(left, right, (((1,), (0,)), ((), ())), preferred_element_type=F32)


def dot_nt(left, right):
    return lax.dot_general(left, right, (((1,), (1,)), ((), ())), preferred_element_type=F32)


def send(src, dst, send_sem, recv_sem, device):
    copy = pltpu.make_async_remote_copy(
        src_ref=src,
        dst_ref=dst,
        send_sem=send_sem,
        recv_sem=recv_sem,
        device_id=device,
        device_id_type=MESH,
    )
    copy.start()
    return copy


class Chunk:
    def __init__(self, width, refs, here):
        self.width = width
        self.part, self.rx, self.sx, self.ry, self.sy, self.rz, self.full, self.ss, self.rs = refs
        self.here = here

    def _wait(self, stage, like, which):
        copy = pltpu.make_async_remote_copy(
            src_ref=like,
            dst_ref=like,
            send_sem=self.ss.at[stage],
            recv_sem=self.rs.at[stage],
            device_id=self.here.mate,
            device_id_type=MESH,
        )
        if which == "recv":
            copy.wait_recv()
        else:
            copy.wait_send()

    def start(self, partial):
        h = self.here
        self.part[...] = partial.astype(BF).reshape(NX, NY, 16, self.width)
        for d in (2, 1, 3):
            send(self.part.at[(h.x + d) % NX], self.rx.at[d - 1], self.ss.at[0], self.rs.at[0], h.at(dx=d))

    def after_x(self):
        h = self.here
        self._wait(0, self.rx, "recv")
        total = self.part[h.x].astype(F32)
        for d in range(NX - 1):
            total += self.rx[d].astype(F32)
        self.sx[...] = total.astype(BF)
        for d in (4, 3, 5, 2, 6, 1, 7):
            send(self.sx.at[(h.y + d) % NY], self.ry.at[d - 1], self.ss.at[1], self.rs.at[1], h.at(dy=d))

    def after_y(self):
        h = self.here
        self._wait(1, self.ry, "recv")
        total = self.sx[h.y].astype(F32)
        for d in range(NY - 1):
            total += self.ry[d].astype(F32)
        self.sy[...] = total.astype(BF)
        for d in (2, 1, 3):
            send(self.sy, self.rz.at[d - 1], self.ss.at[2], self.rs.at[2], h.at(dz=d))

    def after_z(self):
        h = self.here
        self._wait(2, self.rz, "recv")
        total = self.sy[...].astype(F32)
        for d in range(NZ - 1):
            total += self.rz[d].astype(F32)
        self.full[h.x, h.y] = total.astype(BF)
        mine = self.full.at[h.x, h.y]
        for d in (4, 3, 5, 2, 6, 1, 7):
            send(mine, mine, self.ss.at[3], self.rs.at[3], h.at(dy=d))

    def after_gather_y(self):
        h = self.here
        self._wait(3, self.ry, "recv")
        mine = self.full.at[h.x]
        for d in (2, 1, 3):
            send(mine, mine, self.ss.at[4], self.rs.at[4], h.at(dx=d))

    def after_gather_x(self):
        self._wait(4, self.rx, "recv")

    def drain(self):
        self._wait(0, self.rx, "send")
        self._wait(1, self.ry, "send")
        self._wait(2, self.rz, "send")
        self._wait(3, self.ry, "send")
        self._wait(4, self.rx, "send")

    def value(self):
        return self.full[...].reshape(NXI_DEV, self.width)

    def columns(self, j):
        return self.full[:, :, :, j * LANES : (j + 1) * LANES].reshape(NXI_DEV, LANES)


class Here:
    def __init__(self):
        pw, band = lax.axis_index("pw"), lax.axis_index("band")
        self.x, self.z, self.y = pw // (NZ * NY), (pw // NY) % NZ, pw % NY
        self.zh, self.core = band // 2, band % 2
        self.pw = pw
        self.mate = (pw, self.zh * 2 + (1 - self.core))
        self.band = band

    def at(self, dx=0, dy=0, dz=0):
        x, y, z = (self.x + dx) % NX, (self.y + dy) % NY, (self.z + dz) % NZ
        return ((x * NZ + z) * NY + y, self.band)

    def across(self, core):
        return (self.pw, (1 - self.zh) * 2 + core)


def kernel(orb_hbm, xv_hbm, cot_hbm, og_hbm, vg_hbm, *scratch):
    names = ["xv", "xt", "cn", "pn", "cz", "pz", "acc", "vg", "te", "tm", "tl", "tlm", "ts", "ogz", "og"]
    names += ["loc", "ms", "mr", "zs", "zr", "ls", "lr", "es", "er", "fs", "fr", "gs", "gr", "out"]
    s = dict(zip(names, scratch))
    rest = scratch[len(names) :]
    here = Here()
    core = here.core
    per = len(AR_BUFFERS) + 2
    ch = {n: Chunk(w, rest[i * per : (i + 1) * per], here) for i, (n, w) in enumerate(CHUNKS.items())}

    barrier = pltpu.get_barrier_semaphore()
    peers = [here.at(dx=d) for d in (1, 2, 3)] + [here.at(dy=d) for d in range(1, 8)]
    peers += [here.at(dz=d) for d in (1, 2, 3)] + [here.mate, here.across(0), here.across(1)]
    for peer in peers:
        pl.semaphore_signal(barrier, inc=1, device_id=peer, device_id_type=MESH)

    def local(src, dst, sem):
        copy = pltpu.make_async_copy(src, dst, sem)
        copy.start()
        return copy

    loads = []
    for half in range(2):
        rows = pl.ds(half * HALF, HALF)
        loads.append(local(xv_hbm.at[rows], s["xv"].at[rows], s["loc"].at[half]))
    for half in range(2):
        rows = pl.ds(half * HALF, HALF)
        loads.append(local(cot_hbm.at[rows], s["cn"].at[core, half], s["loc"].at[2 + half]))
        loads.append(local(orb_hbm.at[rows], s["pn"].at[core, half], s["loc"].at[4 + half]))
    for load in loads:
        load.wait()
    s["xt"][...] = s["xv"][...].T

    pl.semaphore_wait(barrier, len(peers))

    to_mate = [
        send(s["cn"].at[core], s["cn"].at[core], s["ms"].at[0], s["mr"].at[0], here.mate),
        send(s["pn"].at[core], s["pn"].at[core], s["ms"].at[1], s["mr"].at[1], here.mate),
    ]

    across = here.across(core)

    def send_z(k):
        src, dst = (s["cn"], s["cz"]) if k < 2 else (s["pn"], s["pz"])
        return send(src.at[k % 2, core], dst.at[k % 2, core], s["zs"].at[k], s["zr"].at[k], across)

    def relay(k):
        z_sent[k].wait_recv()
        dst = s["cz"] if k < 2 else s["pz"]
        return send(dst.at[k % 2, core], dst.at[k % 2, core], s["ls"].at[k], s["lr"].at[k], here.mate)

    def panel(name, j):
        return s[name][j].reshape(ROWS, LANES)

    to_mate[0].wait_recv()
    z_sent = [send_z(0), send_z(1)]
    to_mate[1].wait_recv()
    near = jnp.concatenate([panel("cn", 0), panel("cn", 1), panel("pn", 0), panel("pn", 1)], axis=1)
    ch["e"].start(dot_nn(s["xt"][...], near))

    ch["e"].after_x()
    z_sent[0].wait_send()
    z_sent.append(send_z(2))
    relays = [relay(0)]
    relays[0].wait_recv()
    ch["c0"].start(dot_nn(s["xt"][...], panel("cz", 0)))
    ch["e"].after_y()
    z_sent[1].wait_send()
    z_sent.append(send_z(3))
    relays.append(relay(1))
    ch["c0"].after_x()
    relays[1].wait_recv()
    ch["c1"].start(dot_nn(s["xt"][...], panel("cz", 1)))
    ch["e"].after_z()
    ch["c0"].after_y()
    relays.append(relay(2))
    ch["c1"].after_x()
    relays[2].wait_recv()
    ch["p0"].start(dot_nn(s["xt"][...], panel("pz", 0)))
    ch["c0"].after_z()
    ch["e"].after_gather_y()
    ch["c1"].after_y()
    relays.append(relay(3))
    ch["c0"].after_gather_y()
    relays[3].wait_recv()
    ch["p1"].start(dot_nn(s["xt"][...], panel("pz", 1)))
    ch["p0"].after_x()
    ch["c1"].after_z()

    terms_m, terms_z = [], []

    def term(j):
        ch[f"c{j}"].after_gather_x()
        value = dot_nn(s["xv"][...], ch[f"c{j}"].value())
        s["tl"][j] = value.astype(BF).reshape(2, HALF, LANES)
        terms_m.append(send(s["tl"].at[j, 1 - core], s["tlm"].at[j], s["fs"].at[j], s["fr"].at[j], here.mate))

    def term_out(j):
        terms_m[j].wait_recv()
        total = s["tl"][j, core].astype(F32) + s["tlm"][j].astype(F32)
        s["ts"][j] = total.astype(BF)
        terms_z.append(send(s["ts"].at[j], s["ogz"].at[core], s["gs"].at[j], s["gr"].at[0], here.across(j)))

    term(0)
    ch["c1"].after_gather_y()
    term_out(0)
    ch["p0"].after_y()
    ch["p1"].after_x()
    ch["e"].after_gather_x()

    for j in range(2):
        s["te"][j] = dot_nn(s["xv"][...], ch["e"].columns(j)).astype(BF)
    to_mate.append(send(s["te"].at[1 - core], s["tm"], s["es"].at[0], s["er"].at[0], here.mate))
    term(1)
    ch["p0"].after_z()
    term_out(1)

    tile = 256

    def rows_of(name, j, i):
        parts = []
        for k in range(tile // 128):
            at = i * tile + k * 128
            parts.append(s[name][j, at // HALF, at % HALF : at % HALF + 128])
        return jnp.concatenate(parts, axis=0)

    for i in range(ROWS // tile):
        left = jnp.concatenate(
            [rows_of("pn", 0, i), rows_of("pn", 1, i), rows_of("cn", 0, i), rows_of("cn", 1, i)], axis=1
        )
        s["acc"][i * tile : (i + 1) * tile] = dot_nt(left, ch["e"].value())
    ch["p1"].after_y()
    ch["p0"].after_gather_y()
    late = jnp.concatenate([ch["c0"].value(), ch["c1"].value()], axis=1)
    for i in range(ROWS // tile):
        left = jnp.concatenate([rows_of("pz", 0, i), rows_of("pz", 1, i)], axis=1)
        s["acc"][i * tile : (i + 1) * tile] += dot_nt(left, late)
    ch["p1"].after_z()
    to_mate[2].wait_recv()
    ch["p1"].after_gather_y()
    ch["p0"].after_gather_x()
    ch["p1"].after_gather_x()

    late = jnp.concatenate([ch["p0"].value(), ch["p1"].value()], axis=1)
    stores = []
    for i in range(ROWS // tile):
        rows = pl.ds(i * tile, tile)
        left = jnp.concatenate([rows_of("cz", 0, i), rows_of("cz", 1, i)], axis=1)
        s["vg"][rows] = (s["acc"][rows] + dot_nt(left, late)).astype(BF)
        stores.append(local(s["vg"].at[rows], vg_hbm.at[rows], s["out"].at[i]))

    copy = pltpu.make_async_remote_copy(
        src_ref=s["ogz"],
        dst_ref=s["ogz"],
        send_sem=s["gs"].at[0],
        recv_sem=s["gr"].at[0],
        device_id=here.mate,
        device_id_type=MESH,
    )
    copy.wait_recv()
    total = s["te"][core].astype(F32) + s["tm"][...].astype(F32) + s["ogz"][...].reshape(ROWS, LANES).astype(F32)
    s["og"][...] = total.astype(BF)
    stores.append(local(s["og"], og_hbm, s["out"].at[ROWS // tile]))

    for copy in to_mate + z_sent[2:] + relays + terms_m + terms_z:
        copy.wait_send()
    for c in ch.values():
        c.drain()
    for store in stores:
        store.wait()


def body(orbitals, exchange_vectors, cotangent):
    panel = pltpu.VMEM((2, 2, HALF, LANES), BF)
    scratch = [
        pltpu.VMEM((ROWS, NXI_DEV), BF),
        pltpu.VMEM((NXI_DEV, ROWS), BF),
        panel,
        panel,
        panel,
        panel,
        pltpu.VMEM((ROWS, NXI_DEV), F32),
        pltpu.VMEM((ROWS, NXI_DEV), BF),
        pltpu.VMEM((2, ROWS, LANES), BF),
        pltpu.VMEM((ROWS, LANES), BF),
        panel,
        pltpu.VMEM((2, HALF, LANES), BF),
        pltpu.VMEM((2, HALF, LANES), BF),
        pltpu.VMEM((2, HALF, LANES), BF),
        pltpu.VMEM((ROWS, LANES), BF),
        DMA((6,)),
        DMA((2,)),
        DMA((2,)),
        DMA((4,)),
        DMA((4,)),
        DMA((4,)),
        DMA((4,)),
        DMA((1,)),
        DMA((1,)),
        DMA((2,)),
        DMA((2,)),
        DMA((2,)),
        DMA((1,)),
        DMA((6,)),
    ]
    for width in CHUNKS.values():
        scratch += [
            pltpu.VMEM((NX, NY, 16, width), BF),
            pltpu.VMEM((NX - 1, NY, 16, width), BF),
            pltpu.VMEM((NY, 16, width), BF),
            pltpu.VMEM((NY - 1, 16, width), BF),
            pltpu.VMEM((16, width), BF),
            pltpu.VMEM((NZ - 1, 16, width), BF),
            pltpu.VMEM((NX, NY, 16, width), BF),
            DMA((N_STAGES,)),
            DMA((N_STAGES,)),
        ]
    anywhere = pl.BlockSpec(memory_space=pl.ANY)
    return pl.pallas_call(
        kernel,
        out_shape=(
            jax.ShapeDtypeStruct((ROWS, LANES), BF),
            jax.ShapeDtypeStruct((ROWS, NXI_DEV), BF),
        ),
        in_specs=[anywhere] * 3,
        out_specs=(anywhere, anywhere),
        scratch_shapes=scratch,
        name="exchange_backward",
        compiler_params=pltpu.CompilerParams(
            collective_id=0, has_side_effects=True, vmem_limit_bytes=48 << 20
        ),
        cost_estimate=pl.CostEstimate(flops=3400000000, bytes_accessed=4000000, transcendentals=0),
    )(orbitals, exchange_vectors, cotangent)


def solution(mesh):
    placed = (P("pw", "band"), P("pw", "band"), P("pw", "band"))
    return jax.shard_map(
        body,
        mesh=mesh,
        in_specs=placed,
        out_specs=(P("pw", "band"), P("pw", "band")),
        check_vma=False,
    )
```

time: 891 us -> 99.2 us (0.11)
  blocking collectives: 633 us -> 0 us
  waiting for transfers between devices: 227 us -> 0 us
  Pallas kernels: 0 us -> 93 us
  between operations: 13.8 us -> 0.65 us
  matrix products: 11.7 us -> 0 us
    psum x1 -> x0, blocking collectives: 633 us -> none  [body(): summed = lax.psum(partial_terms, 'pw').astype(jnp.bfloat16)]
    reduce_scatter x1 -> x0, waiting for transfers between devices: 147 us -> none  [body(): lax.psum_scatter(local_terms.astype(jnp.bfloat16), 'band', scatter_dimens...]
    pallas_call x0 -> x1, Pallas kernels: none -> 93 us  [body(): pl.pallas_call(kernel, out_shape=(jax.ShapeDtypeStruct((ROWS, LANES), BF)...]
    all_gather x2 -> x0, waiting for transfers between devices: 78.2 us -> none  [the longest x1 45.2 us: body(): lax.all_gather(cotangent, 'band', axis=1, tiled=True)]
    dot_general x5 -> x0, matrix products: 11.7 us -> none  [the longest x2 5.47 us: contract_rows(): lax.dot_general(left, right, (((0,), (0,)), ((), ())), preferred_element_...]
  transfers between devices with their start and end apart: 3 -> 0, of which waited for: 3 -> 0; matrix products, arithmetic and copies ran while one was open for 1% -> 0% of each run, Pallas kernels for 0% -> 0%
where the time goes in v1:
time: 99.2 us; the launch traced here: 98.7 us
  Pallas kernels  93 us (94%)
  local copies, waits for them, and re-layouts  5.04 us (5%)
    pallas_call x1, Pallas kernels, body(): pl.pallas_call(kernel, out_shape=(jax.ShapeDtypeStruct((ROWS, LANES), BF)...  93 us
    unnamed x8, local copies, waits for them, and re-layouts  5.04 us

profile of v1, /device:TPU:1, one launch (start us, length us, event | category | flops | bytes accessed | tf_op | source)
XLA Modules:
  0.0 98.7 jit_solution(17793587097737062604)
XLA Ops:
  0.6 0.0 copy-start
  0.6 1.3 %copy-done = bf16[1280,512]{1,0:T(8,128)(2,1)S(1)} copy-done((bf16[1280,512]{1,0:T(8,128)(2,1)S(1)}, bf16[1280,512]{1,0:T(8,128)(2,1)}, u32[]{:S(2)}) %copy-start) | copy-done | bytes 1310744
  1.9 0.0 copy-start.1
  1.9 1.0 copy-done.1
  2.9 0.0 copy-start.2
  2.9 1.0 copy-done.2
  3.9 93.0 %exchange_backward.1 = (bf16[1280,128]{1,0:T(8,128)(2,1)S(1)}, bf16[1280,512]{1,0:T(8,128)(2,1)S(1)}) custom-call(bf16[1280,128]{1,0:T(8,128)(2,1)S(1)} %copy-done.1, bf16[1280,512]{1,0:T(8,128)(2,1)S(1)} %copy-done, bf16[1280,128]{1,0:T(8,128)(2,1)S(1)} %copy-done.2), custom_call_target="tpu_custom_call" | custom-call | flops 3400000000 | bytes 4000000 | tf_op jit(solution)/shard_map/exchange_backward/pallas_call | solution.py:355
  96.9 0.7 copy.7
  97.7 1.1 %copy.8 = bf16[1280,512]{1,0:T(8,128)(2,1)} copy(bf16[1280,512]{1,0:T(8,128)(2,1)S(1)} %get-tuple-element.5) | data formatting | bytes 2621440
Async XLA Ops:
  0.6 1.3 %copy-start = (bf16[1280,512]{1,0:T(8,128)(2,1)S(1)}, bf16[1280,512]{1,0:T(8,128)(2,1)}, u32[]{:S(2)}) copy-start(bf16[1280,512]{1,0:T(8,128)(2,1)} %xv_hbm.1) | copy-start | bytes 3932164
  1.9 1.0 copy-start.1
  2.9 1.0 copy-start.2

commit v2 on v1

v2 whole, which is shorter than its diff:
```python
import jax
import jax.numpy as jnp
from jax import lax
from jax.experimental import pallas as pl
from jax.experimental.pallas import tpu as pltpu
from jax.sharding import PartitionSpec as P

MESH = pl.DeviceIdType.MESH
BF, F32 = jnp.bfloat16, jnp.float32
NX, NY, NZ = 4, 8, 4
ROWS, HALF, NXI_DEV, LANES = 1280, 640, 512, 128
DMA = pltpu.SemaphoreType.DMA
CHUNKS = {"e": 512, "c0": 128, "c1": 128, "p": 256}
AR_BUFFERS = ("part", "rx", "sx", "ry", "sy", "rz", "full")
N_STAGES = 5


def dot_tn(left, right):
    return lax.dot_general(left, right, (((0,), (0,)), ((), ())), preferred_element_type=F32)


def dot_nn(left, right):
    return lax.dot_general(left, right, (((1,), (0,)), ((), ())), preferred_element_type=F32)


def dot_nt(left, right):
    return lax.dot_general(left, right, (((1,), (1,)), ((), ())), preferred_element_type=F32)


def send(src, dst, send_sem, recv_sem, device):
    copy = pltpu.make_async_remote_copy(
        src_ref=src,
        dst_ref=dst,
        send_sem=send_sem,
        recv_sem=recv_sem,
        device_id=device,
        device_id_type=MESH,
    )
    copy.start()
    return copy


class Chunk:
    def __init__(self, width, refs, here):
        self.width = width
        self.part, self.rx, self.sx, self.ry, self.sy, self.rz, self.full, self.ss, self.rs = refs
        self.here = here

    def _wait(self, stage, like, which):
        copy = pltpu.make_async_remote_copy(
            src_ref=like,
            dst_ref=like,
            send_sem=self.ss.at[stage],
            recv_sem=self.rs.at[stage],
            device_id=self.here.mate,
            device_id_type=MESH,
        )
        if which == "recv":
            copy.wait_recv()
        else:
            copy.wait_send()

    def start(self, partial):
        h = self.here
        self.part[...] = partial.astype(BF).reshape(NX, NY, 16, self.width)
        for d in (2, 1, 3):
            send(self.part.at[(h.x + d) % NX], self.rx.at[d - 1], self.ss.at[0], self.rs.at[0], h.at(dx=d))

    def after_x(self):
        h = self.here
        self._wait(0, self.rx, "recv")
        total = self.part[h.x].astype(F32)
        for d in range(NX - 1):
            total += self.rx[d].astype(F32)
        self.sx[...] = total.astype(BF)
        for d in (4, 3, 5, 2, 6, 1, 7):
            send(self.sx.at[(h.y + d) % NY], self.ry.at[d - 1], self.ss.at[1], self.rs.at[1], h.at(dy=d))

    def after_y(self):
        h = self.here
        self._wait(1, self.ry, "recv")
        total = self.sx[h.y].astype(F32)
        for d in range(NY - 1):
            total += self.ry[d].astype(F32)
        self.sy[...] = total.astype(BF)
        for d in (2, 1, 3):
            send(self.sy, self.rz.at[d - 1], self.ss.at[2], self.rs.at[2], h.at(dz=d))

    def after_z(self):
        h = self.here
        self._wait(2, self.rz, "recv")
        total = self.sy[...].astype(F32)
        for d in range(NZ - 1):
            total += self.rz[d].astype(F32)
        self.full[h.x, h.y] = total.astype(BF)
        mine = self.full.at[h.x, h.y]
        for d in (4, 3, 5, 2, 6, 1, 7):
            send(mine, mine, self.ss.at[3], self.rs.at[3], h.at(dy=d))

    def after_gather_y(self):
        h = self.here
        self._wait(3, self.ry, "recv")
        mine = self.full.at[h.x]
        for d in (2, 1, 3):
            send(mine, mine, self.ss.at[4], self.rs.at[4], h.at(dx=d))

    def after_gather_x(self):
        self._wait(4, self.rx, "recv")

    def drain(self):
        self._wait(0, self.rx, "send")
        self._wait(1, self.ry, "send")
        self._wait(2, self.rz, "send")
        self._wait(3, self.ry, "send")
        self._wait(4, self.rx, "send")

    def value(self):
        return self.full[...].reshape(NXI_DEV, self.width)

    def columns(self, j):
        return self.full[:, :, :, j * LANES : (j + 1) * LANES].reshape(NXI_DEV, LANES)


class Here:
    def __init__(self):
        pw, band = lax.axis_index("pw"), lax.axis_index("band")
        self.x, self.z, self.y = pw // (NZ * NY), (pw // NY) % NZ, pw % NY
        self.zh, self.core = band // 2, band % 2
        self.mate = (pw, self.zh * 2 + (1 - self.core))
        self.pw = pw
        self.band = band

    def at(self, dx=0, dy=0, dz=0):
        x, y, z = (self.x + dx) % NX, (self.y + dy) % NY, (self.z + dz) % NZ
        return ((x * NZ + z) * NY + y, self.band)

    def across(self, core):
        return (self.pw, (1 - self.zh) * 2 + core)


SCRATCH = ("xv", "cn", "pn", "cz", "pz", "acc", "te", "tm", "tz", "tzm", "ts", "ogz")
SEMS = {"load": 3, "ms": 3, "mr": 3, "zs": 3, "zr": 3, "ls": 3, "lr": 3}
SEMS.update({"es": 1, "er": 1, "fs": 2, "fr": 2, "gs": 2, "gr": 1})
PIECES = (8, 2)


def kernel(orb_hbm, xv_hbm, cot_hbm, og, vg, *scratch):
    names = SCRATCH + tuple(SEMS)
    s = dict(zip(names, scratch))
    rest = scratch[len(names) :]
    here = Here()
    per = len(AR_BUFFERS) + 2
    ch = {n: Chunk(w, rest[i * per : (i + 1) * per], here) for i, (n, w) in enumerate(CHUNKS.items())}
    e, p, late = ch["e"], ch["p"], (ch["c0"], ch["c1"])
    core = here.core
    xv, cn, pn, cz, pz = s["xv"], s["cn"], s["pn"], s["cz"], s["pz"]

    barrier = pltpu.get_barrier_semaphore()
    peers = [here.across(0), here.across(1)] + [here.at(dy=d) for d in range(1, 8)] + [here.at(dx=d) for d in (1, 2, 3)]
    peers += [here.at(dz=d) for d in (1, 2, 3)] + [here.mate]
    for peer in peers:
        pl.semaphore_signal(barrier, inc=1, device_id=peer, device_id_type=MESH)

    loads = [
        pltpu.make_async_copy(cot_hbm, cn.at[0], s["load"].at[0]),
        pltpu.make_async_copy(orb_hbm, pn.at[0], s["load"].at[1]),
        pltpu.make_async_copy(xv_hbm, xv, s["load"].at[2]),
    ]
    for load in loads:
        load.start()
    loads[0].wait()
    loads[1].wait()
    pl.semaphore_wait(barrier, len(peers))

    def remote(src, dst, kind, k, device):
        return send(src, dst, s[kind + "s"].at[k], s[kind + "r"].at[k], device)

    def waiter(like, kind, k):
        return pltpu.make_async_remote_copy(
            src_ref=like,
            dst_ref=like,
            send_sem=s[kind + "s"].at[k],
            recv_sem=s[kind + "r"].at[k],
            device_id=here.mate,
            device_id_type=MESH,
        )

    opposite = here.across(core)
    mine, others = pl.ds(core * HALF, HALF), pl.ds((1 - core) * HALF, HALF)
    m_cot = [
        remote(cn.at[0, others], cn.at[1, others], "m", 0, here.mate),
        remote(cn.at[0, mine], cn.at[1, mine], "m", 1, here.mate),
    ]
    m_orb = remote(pn.at[0], pn.at[1], "m", 2, here.mate)
    m_cot[0].wait_recv()
    for j in range(2):
        size = HALF // PIECES[j]
        for i in range(PIECES[j]):
            rows = pl.ds(core * HALF + i * size, size)
            remote(cn.at[(core + j) % 2, rows], cz.at[j, rows], "z", j, opposite)
    z_cot = [waiter(cz.at[j, mine], "z", j) for j in range(2)]
    loads[2].wait()
    m_cot[1].wait_recv()
    m_orb.wait_recv()
    e.start(dot_tn(xv[...], jnp.concatenate([cn[0], cn[1], pn[0], pn[1]], axis=1)))
    e.after_x()
    z_cot[0].wait_send()
    z_orb = remote(pn.at[0], pz.at[core], "z", 2, opposite)

    def relay(j):
        z_cot[j].wait_recv()
        return remote(cz.at[j, mine], cz.at[j, mine], "l", j, here.mate)

    def start_late(j):
        l_cot[j].wait_recv()
        late[j].start(dot_tn(xv[...], cz[j]))

    terms_m, terms_z = [], []

    def term(j):
        s["tz"][j] = dot_nn(xv[...], late[j].value()).astype(BF)
        terms_m.append(remote(s["tz"].at[j, others], s["tzm"].at[j], "f", j, here.mate))

    def term_out(j):
        terms_m[j].wait_recv()
        s["ts"][j] = (s["tz"][j, mine].astype(F32) + s["tzm"][j].astype(F32)).astype(BF)
        terms_z.append(send(s["ts"].at[j], s["ogz"].at[mine], s["gs"].at[j], s["gr"].at[0], here.across(j)))

    l_cot = [relay(0)]
    start_late(0)
    e.after_y()
    late[0].after_x()
    l_cot.append(relay(1))
    start_late(1)
    late[0].after_y()
    late[1].after_x()
    late[0].after_z()
    late[1].after_y()
    z_orb.wait_recv()
    l_orb = remote(pz.at[core], pz.at[core], "l", 2, here.mate)
    late[0].after_gather_y()
    l_orb.wait_recv()
    p.start(dot_tn(xv[...], jnp.concatenate([pz[0], pz[1]], axis=1)))
    late[1].after_z()
    late[0].after_gather_x()
    term(0)
    p.after_x()
    e.after_z()
    term_out(0)
    late[1].after_gather_y()
    e.after_gather_y()
    p.after_y()
    late[1].after_gather_x()
    term(1)
    term_out(1)

    tile = 256
    tiles = [pl.ds(i * tile, tile) for i in range(ROWS // tile)]
    cproj = jnp.concatenate([late[0].value(), late[1].value()], axis=1)
    for rows in tiles:
        left = jnp.concatenate([pz[0, rows], pz[1, rows]], axis=1)
        s["acc"][rows] = dot_nt(left, cproj)
    p.after_z()
    e.after_gather_x()

    for j in range(2):
        s["te"][1 - j] = dot_nn(xv[...], e.columns(1 - j)).astype(BF)
        if j == 0:
            m_term = remote(s["te"].at[1], s["tm"], "e", 0, here.mate)
    p.after_gather_y()
    for rows in tiles:
        left = jnp.concatenate([pn[0, rows], pn[1, rows], cn[0, rows], cn[1, rows]], axis=1)
        s["acc"][rows] += dot_nt(left, e.value())
    m_term.wait_recv()
    p.after_gather_x()
    for rows in tiles:
        left = jnp.concatenate([cz[0, rows], cz[1, rows]], axis=1)
        vg[rows] = (s["acc"][rows] + dot_nt(left, p.value())).astype(BF)

    waiter(s["ogz"], "g", 0).wait_recv()
    total = s["te"][0].astype(F32) + s["tm"][...].astype(F32) + s["ogz"][...].astype(F32)
    og[...] = total.astype(BF)

    for copy in m_cot + [m_orb, z_cot[1], z_orb, l_orb, m_term] + l_cot + terms_m + terms_z:
        copy.wait_send()
    for chunk in ch.values():
        chunk.drain()


def body(orbitals, exchange_vectors, cotangent):
    panels = pltpu.VMEM((2, ROWS, LANES), BF)
    one = pltpu.VMEM((ROWS, LANES), BF)
    halves = pltpu.VMEM((2, HALF, LANES), BF)
    shapes = {
        "xv": pltpu.VMEM((ROWS, NXI_DEV), BF),
        "cn": panels,
        "pn": panels,
        "cz": panels,
        "pz": panels,
        "acc": pltpu.VMEM((ROWS, NXI_DEV), F32),
        "te": panels,
        "tm": one,
        "tz": panels,
        "tzm": halves,
        "ts": halves,
        "ogz": one,
    }
    scratch = [shapes[name] for name in SCRATCH] + [DMA((n,)) for n in SEMS.values()]
    for width in CHUNKS.values():
        scratch += [
            pltpu.VMEM((NX, NY, 16, width), BF),
            pltpu.VMEM((NX - 1, NY, 16, width), BF),
            pltpu.VMEM((NY, 16, width), BF),
            pltpu.VMEM((NY - 1, 16, width), BF),
            pltpu.VMEM((16, width), BF),
            pltpu.VMEM((NZ - 1, 16, width), BF),
            pltpu.VMEM((NX, NY, 16, width), BF),
            DMA((N_STAGES,)),
            DMA((N_STAGES,)),
        ]
    return pl.pallas_call(
        kernel,
        out_shape=(
            jax.ShapeDtypeStruct((ROWS, LANES), BF),
            jax.ShapeDtypeStruct((ROWS, NXI_DEV), BF),
        ),
        in_specs=[pl.BlockSpec(memory_space=pltpu.HBM)] * 3,
        out_specs=(pl.BlockSpec(memory_space=pltpu.VMEM), pl.BlockSpec(memory_space=pltpu.VMEM)),
        scratch_shapes=scratch,
        name="exchange_backward",
        compiler_params=pltpu.CompilerParams(
            collective_id=0, has_side_effects=True, vmem_limit_bytes=205 << 18
        ),
        cost_estimate=pl.CostEstimate(flops=3400000000, bytes_accessed=4000000, transcendentals=0),
    )(orbitals, exchange_vectors, cotangent)


def solution(mesh):
    placed = (P("pw", "band"), P("pw", "band"), P("pw", "band"))
    return jax.shard_map(
        body,
        mesh=mesh,
        in_specs=placed,
        out_specs=(P("pw", "band"), P("pw", "band")),
        check_vma=False,
    )
```

time: 99.2 us -> 90.1 us (0.908)
  the two profiles are of different devices: /device:TPU:1 before, /device:TPU:2 now
where the time goes in v2:
time: 90.1 us; the launch traced here: 89.9 us
  Pallas kernels  85.5 us (95%)
  local copies, waits for them, and re-layouts  3.72 us (4%)
    pallas_call x1, Pallas kernels, body(): pl.pallas_call(kernel, out_shape=(jax.ShapeDtypeStruct((ROWS, LANES), BF)...  85.5 us
    unnamed x6, local copies, waits for them, and re-layouts  3.72 us

profile of v2, /device:TPU:2, one launch (start us, length us, event | category | flops | bytes accessed | tf_op | source)
XLA Modules:
  0.0 89.9 jit_solution(5729974426556342689)
XLA Ops:
  0.6 0.0 copy-start
  0.6 1.0 %copy-done = bf16[1280,128]{1,0:T(8,128)(2,1)S(1)} copy-done((bf16[1280,128]{1,0:T(8,128)(2,1)S(1)}, bf16[1280,128]{1,0:T(8,128)(2,1)}, u32[]{:S(2)}) %copy-start) | copy-done | bytes 327704
  1.6 0.0 copy-start.1
  1.6 1.0 %copy-done.1 = bf16[1280,128]{1,0:T(8,128)(2,1)S(1)} copy-done((bf16[1280,128]{1,0:T(8,128)(2,1)S(1)}, bf16[1280,128]{1,0:T(8,128)(2,1)}, u32[]{:S(2)}) %copy-start.1) | copy-done | bytes 327704
  2.6 85.5 %exchange_backward.1 = (bf16[1280,128]{1,0:T(8,128)(2,1)S(1)}, bf16[1280,512]{1,0:T(8,128)(2,1)S(1)}) custom-call(bf16[1280,128]{1,0:T(8,128)(2,1)S(1)} %copy-done, bf16[1280,512]{1,0:T(8,128)(2,1)} %xv_hbm.1, bf16[1280,128]{1,0:T(8,128)(2,1)S(1)} %copy-done.1), custom_call_target="tpu_custom_call" | custom-call | flops 3400000000 | bytes 4000000 | tf_op jit(solution)/shard_map/exchange_backward/pallas_call | solution.py:321
  88.1 0.7 copy.7
  88.8 1.1 %copy.8 = bf16[1280,512]{1,0:T(8,128)(2,1)} copy(bf16[1280,512]{1,0:T(8,128)(2,1)S(1)} %get-tuple-element.5) | data formatting | bytes 2621440
Async XLA Ops:
  0.6 1.0 %copy-start = (bf16[1280,128]{1,0:T(8,128)(2,1)S(1)}, bf16[1280,128]{1,0:T(8,128)(2,1)}, u32[]{:S(2)}) copy-start(bf16[1280,128]{1,0:T(8,128)(2,1)} %orb_hbm.1) | copy-start | bytes 983044
  1.6 1.0 %copy-start.1 = (bf16[1280,128]{1,0:T(8,128)(2,1)S(1)}, bf16[1280,128]{1,0:T(8,128)(2,1)}, u32[]{:S(2)}) copy-start(bf16[1280,128]{1,0:T(8,128)(2,1)} %cot_hbm.1) | copy-start | bytes 983044

commit v3 on v2

--- a/solution.py
+++ b/solution.py
@@ -13,6 +13,7 @@
 CHUNKS = {"e": 512, "c0": 128, "c1": 128, "p": 256}
 AR_BUFFERS = ("part", "rx", "sx", "ry", "sy", "rz", "full")
 N_STAGES = 5
+TILE = 256
 
 
 def dot_tn(left, right):
@@ -202,81 +203,83 @@
     loads[2].wait()
     m_cot[1].wait_recv()
     m_orb.wait_recv()
+    def relay(j):
+        z_cot[j].wait_recv()
+        return remote(cz.at[j, mine], cz.at[j, mine], "l", j, here.mate)
+
+    def start_late(j):
+        l_cot[j].wait_recv()
+        late[j].start(dot_tn(xv[...], cz[j]))
+
+    terms_m, terms_z = [], []
+
+    def term(j):
+        s["tz"][j] = dot_nn(xv[...], late[j].value()).astype(BF)
+        terms_m.append(remote(s["tz"].at[j, others], s["tzm"].at[j], "f", j, here.mate))
+
+    def term_out(j):
+        terms_m[j].wait_recv()
+        s["ts"][j] = (s["tz"][j, mine].astype(F32) + s["tzm"][j].astype(F32)).astype(BF)
+        terms_z.append(send(s["ts"].at[j], s["ogz"].at[mine], s["gs"].at[j], s["gr"].at[0], here.across(j)))
+
+
+    tiles = [pl.ds(i * TILE, TILE) for i in range(ROWS // TILE)]
+    added = []
+
+    def add_to_grad(panels, right, last=False):
+        for rows in tiles:
+            total = dot_nt(jnp.concatenate([ref[k, rows] for ref, k in panels], axis=1), right)
+            if added:
+                total += s["acc"][rows]
+            if last:
+                vg[rows] = total.astype(BF)
+            else:
+                s["acc"][rows] = total
+        added.append(right)
+
     e.start(dot_tn(xv[...], jnp.concatenate([cn[0], cn[1], pn[0], pn[1]], axis=1)))
     e.after_x()
     z_cot[0].wait_send()
     z_orb = remote(pn.at[0], pz.at[core], "z", 2, opposite)
-
-    def relay(j):
-        z_cot[j].wait_recv()
-        return remote(cz.at[j, mine], cz.at[j, mine], "l", j, here.mate)
-
-    def start_late(j):
-        l_cot[j].wait_recv()
-        late[j].start(dot_tn(xv[...], cz[j]))
-
-    terms_m, terms_z = [], []
-
-    def term(j):
-        s["tz"][j] = dot_nn(xv[...], late[j].value()).astype(BF)
-        terms_m.append(remote(s["tz"].at[j, others], s["tzm"].at[j], "f", j, here.mate))
-
-    def term_out(j):
-        terms_m[j].wait_recv()
-        s["ts"][j] = (s["tz"][j, mine].astype(F32) + s["tzm"][j].astype(F32)).astype(BF)
-        terms_z.append(send(s["ts"].at[j], s["ogz"].at[mine], s["gs"].at[j], s["gr"].at[0], here.across(j)))
-
     l_cot = [relay(0)]
+    l_cot.append(relay(1))
     start_late(0)
+    start_late(1)
+    late[0].after_x()
+    late[1].after_x()
+    late[0].after_y()
     e.after_y()
-    late[0].after_x()
-    l_cot.append(relay(1))
-    start_late(1)
-    late[0].after_y()
-    late[1].after_x()
-    late[0].after_z()
-    late[1].after_y()
     z_orb.wait_recv()
     l_orb = remote(pz.at[core], pz.at[core], "l", 2, here.mate)
-    late[0].after_gather_y()
+    late[1].after_y()
+    late[0].after_z()
     l_orb.wait_recv()
     p.start(dot_tn(xv[...], jnp.concatenate([pz[0], pz[1]], axis=1)))
     late[1].after_z()
+    late[0].after_gather_y()
+    p.after_x()
+    e.after_z()
     late[0].after_gather_x()
     term(0)
-    p.after_x()
-    e.after_z()
+    late[1].after_gather_y()
+    p.after_y()
     term_out(0)
-    late[1].after_gather_y()
+    p.after_z()
     e.after_gather_y()
-    p.after_y()
     late[1].after_gather_x()
+    add_to_grad([(pz, 0), (pz, 1)], jnp.concatenate([late[0].value(), late[1].value()], axis=1))
     term(1)
     term_out(1)
-
-    tile = 256
-    tiles = [pl.ds(i * tile, tile) for i in range(ROWS // tile)]
-    cproj = jnp.concatenate([late[0].value(), late[1].value()], axis=1)
-    for rows in tiles:
-        left = jnp.concatenate([pz[0, rows], pz[1, rows]], axis=1)
-        s["acc"][rows] = dot_nt(left, cproj)
-    p.after_z()
+    p.after_gather_y()
     e.after_gather_x()
-
-    for j in range(2):
-        s["te"][1 - j] = dot_nn(xv[...], e.columns(1 - j)).astype(BF)
-        if j == 0:
+    add_to_grad([(pn, 0), (pn, 1), (cn, 0), (cn, 1)], e.value())
+    for k in (1, 0):
+        s["te"][k] = dot_nn(xv[...], e.columns(k)).astype(BF)
+        if k == 1:
             m_term = remote(s["te"].at[1], s["tm"], "e", 0, here.mate)
-    p.after_gather_y()
-    for rows in tiles:
-        left = jnp.concatenate([pn[0, rows], pn[1, rows], cn[0, rows], cn[1, rows]], axis=1)
-        s["acc"][rows] += dot_nt(left, e.value())
+    p.after_gather_x()
+    add_to_grad([(cz, 0), (cz, 1)], p.value(), last=True)
     m_term.wait_recv()
-    p.after_gather_x()
-    for rows in tiles:
-        left = jnp.concatenate([cz[0, rows], cz[1, rows]], axis=1)
-        vg[rows] = (s["acc"][rows] + dot_nt(left, p.value())).astype(BF)
-
     waiter(s["ogz"], "g", 0).wait_recv()
     total = s["te"][0].astype(F32) + s["tm"][...].astype(F32) + s["ogz"][...].astype(F32)
     og[...] = total.astype(BF)

time: 90.1 us -> 87.6 us (0.972)
  the two profiles are of different devices: /device:TPU:2 before, /device:TPU:128 now
where the time goes in v3:
time: 87.6 us; the launch traced here: 87.4 us
  Pallas kernels  83 us (95%)
  local copies, waits for them, and re-layouts  3.72 us (4%)
    pallas_call x1, Pallas kernels, body(): pl.pallas_call(kernel, out_shape=(jax.ShapeDtypeStruct((ROWS, LANES), BF)...  83 us
    unnamed x6, local copies, waits for them, and re-layouts  3.72 us

profile of v3, /device:TPU:128, one launch (start us, length us, event | category | flops | bytes accessed | tf_op | source)
XLA Modules:
  0.0 87.4 jit_solution(7803507722059698859)
XLA Ops:
  0.6 0.0 copy-start
  0.6 1.0 %copy-done = bf16[1280,128]{1,0:T(8,128)(2,1)S(1)} copy-done((bf16[1280,128]{1,0:T(8,128)(2,1)S(1)}, bf16[1280,128]{1,0:T(8,128)(2,1)}, u32[]{:S(2)}) %copy-start) | copy-done | bytes 327704
  1.6 0.0 copy-start.1
  1.6 1.0 %copy-done.1 = bf16[1280,128]{1,0:T(8,128)(2,1)S(1)} copy-done((bf16[1280,128]{1,0:T(8,128)(2,1)S(1)}, bf16[1280,128]{1,0:T(8,128)(2,1)}, u32[]{:S(2)}) %copy-start.1) | copy-done | bytes 327704
  2.6 83.0 %exchange_backward.1 = (bf16[1280,128]{1,0:T(8,128)(2,1)S(1)}, bf16[1280,512]{1,0:T(8,128)(2,1)S(1)}) custom-call(bf16[1280,128]{1,0:T(8,128)(2,1)S(1)} %copy-done, bf16[1280,512]{1,0:T(8,128)(2,1)} %xv_hbm.1, bf16[1280,128]{1,0:T(8,128)(2,1)S(1)} %copy-done.1), custom_call_target="tpu_custom_call" | custom-call | flops 3400000000 | bytes 4000000 | tf_op jit(solution)/shard_map/exchange_backward/pallas_call | solution.py:324
  85.6 0.7 copy.7
  86.3 1.1 %copy.8 = bf16[1280,512]{1,0:T(8,128)(2,1)} copy(bf16[1280,512]{1,0:T(8,128)(2,1)S(1)} %get-tuple-element.5) | data formatting | bytes 2621440
Async XLA Ops:
  0.6 1.0 %copy-start = (bf16[1280,128]{1,0:T(8,128)(2,1)S(1)}, bf16[1280,128]{1,0:T(8,128)(2,1)}, u32[]{:S(2)}) copy-start(bf16[1280,128]{1,0:T(8,128)(2,1)} %orb_hbm.1) | copy-start | bytes 983044
  1.6 1.0 %copy-start.1 = (bf16[1280,128]{1,0:T(8,128)(2,1)S(1)}, bf16[1280,128]{1,0:T(8,128)(2,1)}, u32[]{:S(2)}) copy-start(bf16[1280,128]{1,0:T(8,128)(2,1)} %cot_hbm.1) | copy-start | bytes 983044

commit v4 on v3

--- a/solution.py
+++ b/solution.py
@@ -10,7 +10,7 @@
 NX, NY, NZ = 4, 8, 4
 ROWS, HALF, NXI_DEV, LANES = 1280, 640, 512, 128
 DMA = pltpu.SemaphoreType.DMA
-CHUNKS = {"e": 512, "c0": 128, "c1": 128, "p": 256}
+CHUNKS = {"e": 512, "c0": 128, "c1": 128, "p0": 128, "p1": 128}
 AR_BUFFERS = ("part", "rx", "sx", "ry", "sy", "rz", "full")
 N_STAGES = 5
 TILE = 256
@@ -140,7 +140,7 @@
 
 
 SCRATCH = ("xv", "cn", "pn", "cz", "pz", "acc", "te", "tm", "tz", "tzm", "ts", "ogz")
-SEMS = {"load": 3, "ms": 3, "mr": 3, "zs": 3, "zr": 3, "ls": 3, "lr": 3}
+SEMS = {"load": 3, "ms": 3, "mr": 3, "zs": 4, "zr": 4, "ls": 4, "lr": 4}
 SEMS.update({"es": 1, "er": 1, "fs": 2, "fr": 2, "gs": 2, "gr": 1})
 PIECES = (8, 2)
 
@@ -152,7 +152,7 @@
     here = Here()
     per = len(AR_BUFFERS) + 2
     ch = {n: Chunk(w, rest[i * per : (i + 1) * per], here) for i, (n, w) in enumerate(CHUNKS.items())}
-    e, p, late = ch["e"], ch["p"], (ch["c0"], ch["c1"])
+    e, late, last = ch["e"], (ch["c0"], ch["c1"]), (ch["p0"], ch["p1"])
     core = here.core
     xv, cn, pn, cz, pz = s["xv"], s["cn"], s["pn"], s["cz"], s["pz"]
 
@@ -223,68 +223,87 @@
         terms_z.append(send(s["ts"].at[j], s["ogz"].at[mine], s["gs"].at[j], s["gr"].at[0], here.across(j)))
 
 
+    z_orb = []
+
+    def send_orb(j):
+        z_cot[j].wait_send()
+        z_orb.append(remote(pn.at[(core + j) % 2, mine], pz.at[j, mine], "z", 2 + j, opposite))
+
+    def relay_orb(j):
+        z_orb[j].wait_recv()
+        return remote(pz.at[j, mine], pz.at[j, mine], "l", 2 + j, here.mate)
+
+    def start_last(j):
+        l_orb[j].wait_recv()
+        last[j].start(dot_tn(xv[...], pz[j]))
+
     tiles = [pl.ds(i * TILE, TILE) for i in range(ROWS // TILE)]
     added = []
 
-    def add_to_grad(panels, right, last=False):
+    def add_to_grad(panels, right, final=False):
         for rows in tiles:
             total = dot_nt(jnp.concatenate([ref[k, rows] for ref, k in panels], axis=1), right)
             if added:
                 total += s["acc"][rows]
-            if last:
+            if final:
                 vg[rows] = total.astype(BF)
             else:
                 s["acc"][rows] = total
         added.append(right)
 
     e.start(dot_tn(xv[...], jnp.concatenate([cn[0], cn[1], pn[0], pn[1]], axis=1)))
+    send_orb(0)
+    l_cot = [relay(0)]
     e.after_x()
-    z_cot[0].wait_send()
-    z_orb = remote(pn.at[0], pz.at[core], "z", 2, opposite)
-    l_cot = [relay(0)]
+    start_late(0)
+    send_orb(1)
+    late[0].after_x()
     l_cot.append(relay(1))
-    start_late(0)
     start_late(1)
-    late[0].after_x()
+    l_orb = [relay_orb(0)]
+    start_last(0)
+    e.after_y()
+    late[0].after_y()
     late[1].after_x()
-    late[0].after_y()
-    e.after_y()
-    z_orb.wait_recv()
-    l_orb = remote(pz.at[core], pz.at[core], "l", 2, here.mate)
+    late[0].after_z()
+    l_orb.append(relay_orb(1))
+    last[0].after_x()
+    start_last(1)
     late[1].after_y()
-    late[0].after_z()
-    l_orb.wait_recv()
-    p.start(dot_tn(xv[...], jnp.concatenate([pz[0], pz[1]], axis=1)))
+    e.after_z()
+    late[0].after_gather_y()
+    last[0].after_y()
     late[1].after_z()
-    late[0].after_gather_y()
-    p.after_x()
-    e.after_z()
+    last[1].after_x()
     late[0].after_gather_x()
+    last[0].after_z()
     term(0)
     late[1].after_gather_y()
-    p.after_y()
+    last[1].after_y()
     term_out(0)
-    p.after_z()
     e.after_gather_y()
     late[1].after_gather_x()
-    add_to_grad([(pz, 0), (pz, 1)], jnp.concatenate([late[0].value(), late[1].value()], axis=1))
     term(1)
     term_out(1)
-    p.after_gather_y()
+    last[1].after_z()
+    add_to_grad([(pz, 0), (pz, 1)], jnp.concatenate([late[0].value(), late[1].value()], axis=1))
     e.after_gather_x()
+    last[0].after_gather_y()
     add_to_grad([(pn, 0), (pn, 1), (cn, 0), (cn, 1)], e.value())
+    last[1].after_gather_y()
     for k in (1, 0):
         s["te"][k] = dot_nn(xv[...], e.columns(k)).astype(BF)
         if k == 1:
             m_term = remote(s["te"].at[1], s["tm"], "e", 0, here.mate)
-    p.after_gather_x()
-    add_to_grad([(cz, 0), (cz, 1)], p.value(), last=True)
+    last[0].after_gather_x()
+    last[1].after_gather_x()
+    add_to_grad([(cz, 0), (cz, 1)], jnp.concatenate([last[0].value(), last[1].value()], axis=1), final=True)
     m_term.wait_recv()
     waiter(s["ogz"], "g", 0).wait_recv()
     total = s["te"][0].astype(F32) + s["tm"][...].astype(F32) + s["ogz"][...].astype(F32)
     og[...] = total.astype(BF)
 
-    for copy in m_cot + [m_orb, z_cot[1], z_orb, l_orb, m_term] + l_cot + terms_m + terms_z:
+    for copy in m_cot + [m_orb, m_term] + z_orb + l_orb + l_cot + terms_m + terms_z:
         copy.wait_send()
     for chunk in ch.values():
         chunk.drain()

time: 87.6 us -> 83.6 us (0.954)
  the two profiles are of different devices: /device:TPU:128 before, /device:TPU:1 now
where the time goes in v4:
time: 83.6 us; the launch traced here: 83.3 us
  Pallas kernels  79 us (94%)
  local copies, waits for them, and re-layouts  3.72 us (4%)
    pallas_call x1, Pallas kernels, body(): pl.pallas_call(kernel, out_shape=(jax.ShapeDtypeStruct((ROWS, LANES), BF)...  79 us
    unnamed x6, local copies, waits for them, and re-layouts  3.72 us

profile of v4, /device:TPU:1, one launch (start us, length us, event | category | flops | bytes accessed | tf_op | source)
XLA Modules:
  0.0 83.3 jit_solution(10696140368332184529)
XLA Ops:
  0.6 0.0 copy-start
  0.6 1.0 %copy-done = bf16[1280,128]{1,0:T(8,128)(2,1)S(1)} copy-done((bf16[1280,128]{1,0:T(8,128)(2,1)S(1)}, bf16[1280,128]{1,0:T(8,128)(2,1)}, u32[]{:S(2)}) %copy-start) | copy-done | bytes 327704
  1.6 0.0 copy-start.1
  1.6 1.0 %copy-done.1 = bf16[1280,128]{1,0:T(8,128)(2,1)S(1)} copy-done((bf16[1280,128]{1,0:T(8,128)(2,1)S(1)}, bf16[1280,128]{1,0:T(8,128)(2,1)}, u32[]{:S(2)}) %copy-start.1) | copy-done | bytes 327704
  2.6 79.0 %exchange_backward.1 = (bf16[1280,128]{1,0:T(8,128)(2,1)S(1)}, bf16[1280,512]{1,0:T(8,128)(2,1)S(1)}) custom-call(bf16[1280,128]{1,0:T(8,128)(2,1)S(1)} %copy-done, bf16[1280,512]{1,0:T(8,128)(2,1)} %xv_hbm.1, bf16[1280,128]{1,0:T(8,128)(2,1)S(1)} %copy-done.1), custom_call_target="tpu_custom_call" | custom-call | flops 3400000000 | bytes 4000000 | tf_op jit(solution)/shard_map/exchange_backward/pallas_call | solution.py:343
  81.5 0.7 copy.7
  82.3 1.1 %copy.8 = bf16[1280,512]{1,0:T(8,128)(2,1)} copy(bf16[1280,512]{1,0:T(8,128)(2,1)S(1)} %get-tuple-element.5) | data formatting | bytes 2621440
Async XLA Ops:
  0.6 1.0 %copy-start = (bf16[1280,128]{1,0:T(8,128)(2,1)S(1)}, bf16[1280,128]{1,0:T(8,128)(2,1)}, u32[]{:S(2)}) copy-start(bf16[1280,128]{1,0:T(8,128)(2,1)} %orb_hbm.1) | copy-start | bytes 983044
  1.6 1.0 %copy-start.1 = (bf16[1280,128]{1,0:T(8,128)(2,1)S(1)}, bf16[1280,128]{1,0:T(8,128)(2,1)}, u32[]{:S(2)}) copy-start(bf16[1280,128]{1,0:T(8,128)(2,1)} %cot_hbm.1) | copy-start | bytes 983044

commit v5 on v4

--- a/solution.py
+++ b/solution.py
@@ -256,13 +256,13 @@
     l_cot = [relay(0)]
     e.after_x()
     start_late(0)
+    e.after_y()
     send_orb(1)
     late[0].after_x()
     l_cot.append(relay(1))
     start_late(1)
     l_orb = [relay_orb(0)]
     start_last(0)
-    e.after_y()
     late[0].after_y()
     late[1].after_x()
     late[0].after_z()

time: 83.6 us -> 83.9 us (level)
  the two profiles are of different devices: /device:TPU:1 before, /device:TPU:256 now
where the time goes in v5:
time: 83.9 us; the launch traced here: 83.7 us
  Pallas kernels  79.3 us (95%)
  local copies, waits for them, and re-layouts  3.72 us (4%)
    pallas_call x1, Pallas kernels, body(): pl.pallas_call(kernel, out_shape=(jax.ShapeDtypeStruct((ROWS, LANES), BF)...  79.3 us
    unnamed x6, local copies, waits for them, and re-layouts  3.72 us

profile of v5, /device:TPU:256, one launch (start us, length us, event | category | flops | bytes accessed | tf_op | source)
XLA Modules:
  0.0 83.7 jit_solution(16963279711676571595)
XLA Ops:
  0.6 0.0 copy-start
  0.6 1.0 %copy-done = bf16[1280,128]{1,0:T(8,128)(2,1)S(1)} copy-done((bf16[1280,128]{1,0:T(8,128)(2,1)S(1)}, bf16[1280,128]{1,0:T(8,128)(2,1)}, u32[]{:S(2)}) %copy-start) | copy-done | bytes 327704
  1.6 0.0 copy-start.1
  1.6 1.0 %copy-done.1 = bf16[1280,128]{1,0:T(8,128)(2,1)S(1)} copy-done((bf16[1280,128]{1,0:T(8,128)(2,1)S(1)}, bf16[1280,128]{1,0:T(8,128)(2,1)}, u32[]{:S(2)}) %copy-start.1) | copy-done | bytes 327704
  2.6 79.3 %exchange_backward.1 = (bf16[1280,128]{1,0:T(8,128)(2,1)S(1)}, bf16[1280,512]{1,0:T(8,128)(2,1)S(1)}) custom-call(bf16[1280,128]{1,0:T(8,128)(2,1)S(1)} %copy-done, bf16[1280,512]{1,0:T(8,128)(2,1)} %xv_hbm.1, bf16[1280,128]{1,0:T(8,128)(2,1)S(1)} %copy-done.1), custom_call_target="tpu_custom_call" | custom-call | flops 3400000000 | bytes 4000000 | tf_op jit(solution)/shard_map/exchange_backward/pallas_call | solution.py:343
  81.9 0.7 copy.7
  82.6 1.1 %copy.8 = bf16[1280,512]{1,0:T(8,128)(2,1)} copy(bf16[1280,512]{1,0:T(8,128)(2,1)S(1)} %get-tuple-element.5) | data formatting | bytes 2621440
Async XLA Ops:
  0.6 1.0 %copy-start = (bf16[1280,128]{1,0:T(8,128)(2,1)S(1)}, bf16[1280,128]{1,0:T(8,128)(2,1)}, u32[]{:S(2)}) copy-start(bf16[1280,128]{1,0:T(8,128)(2,1)} %orb_hbm.1) | copy-start | bytes 983044
  1.6 1.0 %copy-start.1 = (bf16[1280,128]{1,0:T(8,128)(2,1)S(1)}, bf16[1280,128]{1,0:T(8,128)(2,1)}, u32[]{:S(2)}) copy-start(bf16[1280,128]{1,0:T(8,128)(2,1)} %cot_hbm.1) | copy-start | bytes 983044
